TPU v7x, 32 devices: a whole 2x2x4 slice. The times are simulated.
32 devices in a mesh: tm: 32 (over z, y, x, core).
Axes of the slice: x: 2, y: 2, z: 4, core: 2. Of those that a mesh axis runs over, the one named last changes fastest.
Arguments:
- inv_diag: float32 [32, 384, 384], P('tm'), may hold values from -0.4 to 4.4, as said below
- low_coupling: float32 [32, 384, 384], P('tm'), may hold values from -0.09375 to 0.09375
- up_coupling: float32 [32, 384, 384], P('tm'), may hold values from -0.09375 to 0.09375
Outputs:
- diag_inverse: float32 [32, 384, 384], P('tm')
- cross_inverse: float32 [32, 384, 384], P('tm')
Inputs may be any that keep to these rules, and one draw needn't show every extreme that they name: `inv_diag`: each block is symmetric.
All inputs are finite; a program needn't handle non-finite values.
Results may differ from a plain program's by a relative error of at most 0.00012.
Values sent between devices are 32-bit elements; how exact they have to be, the bound alone decides.
No kernel may reach another device: no remote copies, remote signals or barrier semaphores. Data moves between devices by JAX's collectives and lax.ppermute only.
A program may use at most 64 MiB of HBM per device.

v0:
```python
import functools

import jax
import jax.numpy as jnp
from jax import lax
from jax.experimental import pallas as pl
from jax.experimental.pallas import tpu as pltpu
from jax.sharding import PartitionSpec as P

row_offset = 3
lanes = 128
group = 8
axis = "tm"
bf16 = jnp.bfloat16
f32 = jnp.float32


def sym_rows(width):
    blocks = width // lanes
    pairs = blocks // 2
    return (blocks * (blocks - 1) // 2 + blocks - pairs) * lanes + 8 * pairs


def full_rows(width):
    return width * (width // lanes)


def tri():
    r = lax.broadcasted_iota(jnp.int32, (lanes, lanes), 0)
    c = lax.broadcasted_iota(jnp.int32, (lanes, lanes), 1)
    return r, c


def put_sym(ref, at, mat):
    blocks = mat.shape[0] // lanes
    block = lambda i, j: mat[i * lanes : (i + 1) * lanes, j * lanes : (j + 1) * lanes]
    for i in range(blocks):
        for j in range(i):
            ref[pl.ds(at, lanes), :] = block(i, j)
            at += lanes
    r, c = tri()
    for i in range(0, blocks - 1, 2):
        one, two = block(i, i), block(i + 1, i + 1)
        ref[pl.ds(at, lanes), :] = jnp.where(r >= c, one, two)
        at += lanes
        line = jnp.sum(jnp.where(r == c, two, 0.0), axis=0, keepdims=True)
        ref[pl.ds(at, 8), :] = jnp.broadcast_to(line, (8, lanes))
        at += 8
    if blocks % 2:
        ref[pl.ds(at, lanes), :] = block(blocks - 1, blocks - 1)


def get_sym(ref, at, width):
    blocks = width // lanes
    got = {}
    for i in range(blocks):
        for j in range(i):
            got[i, j] = ref[pl.ds(at, lanes), :]
            got[j, i] = got[i, j].T
            at += lanes
    r, c = tri()
    for i in range(0, blocks - 1, 2):
        both = ref[pl.ds(at, lanes), :]
        turned = both.T
        at += lanes
        line = ref[pl.ds(at, 8), :][0:1, :]
        at += 8
        got[i, i] = jnp.where(r >= c, both, turned)
        got[i + 1, i + 1] = jnp.where(r == c, line, jnp.where(r < c, both, turned))
    if blocks % 2:
        got[blocks - 1, blocks - 1] = ref[pl.ds(at, lanes), :]
    return jnp.concatenate(
        [jnp.concatenate([got[i, j] for j in range(blocks)], axis=1) for i in range(blocks)], axis=0
    )


def put_full(ref, at, mat):
    width = mat.shape[0]
    for j in range(width // lanes):
        ref[pl.ds(at + j * width, width), :] = mat[:, j * lanes : (j + 1) * lanes]


def get_full(ref, at, width):
    return jnp.concatenate(
        [ref[pl.ds(at + j * width, width), :] for j in range(width // lanes)], axis=1
    )


def parts_of(mat):
    high = mat.astype(bf16)
    return high, (mat - high.astype(f32)).astype(bf16)


def times(left, right, turned=False):
    dims = (((1,), (1 if turned else 0,)), ((), ()))
    dot = lambda a, b: lax.dot_general(a, b, dims, preferred_element_type=f32)
    return dot(left[0], right[0]) + (dot(left[0], right[1]) + dot(left[1], right[0]))


def long_left(parts):
    high, low = parts
    return jnp.concatenate([high, high, low], axis=1)


def long_right(parts, turned=False):
    high, low = parts
    return jnp.concatenate([high, low, high], axis=1 if turned else 0)


def long_times(left, right, turned=False):
    dims = (((1,), (1 if turned else 0,)), ((), ()))
    return lax.dot_general(left, right, dims, preferred_element_type=f32)


def symmetric_times(left, right):
    high, low = left
    width = high.shape[0]
    most = width // (2 * lanes) * (2 * lanes)

    def part(rows, columns):
        both = long_times(jnp.concatenate([high[rows], low[rows]], axis=0), right[0][columns], True)
        count = both.shape[0] // 2
        return (both[:count] + both[count:]) + long_times(high[rows], right[1][columns], True)

    wide = part(slice(0, width), slice(0, most))
    if most == width:
        return wide
    rest = part(slice(most, width), slice(most, width))
    return jnp.concatenate([wide, jnp.concatenate([wide[most:].T, rest], axis=0)], axis=1)


def beside(left, right):
    return tuple(jnp.concatenate(pair, axis=1) for pair in zip(left, right))


def set_state(sh, sl, aa, ba, bb):
    width = aa.shape[0]
    first, second = slice(0, width), slice(width, 2 * width)
    for rows, columns, mat in ((first, first, aa), (second, first, ba), (first, second, ba.T), (second, second, bb)):
        sh[rows, columns], sl[rows, columns] = parts_of(mat)


def eliminate(node, sh, sl):
    diag, g_mat, h_mat = node
    left = parts_of(jnp.concatenate([g_mat, h_mat], axis=1))
    passed = -times(left, (sh[...], sl[...]))
    return passed, diag - symmetric_times(left, parts_of(passed))


def place_now(length):
    return lax.rem(lax.axis_index(axis) + row_offset, length)


def fetch(sems, *pairs):
    copies = [pltpu.make_async_copy(source, target, sems.at[i]) for i, (source, target) in enumerate(pairs)]
    for copy in copies:
        copy.start()
    for copy in copies:
        copy.wait()


def own_kernel(inv_ref, low_ref, up_ref, sym_ref, g_ref, node_ref, rooms, lines, sems, out_sems):
    width = inv_ref.shape[1]
    ps, pf = sym_rows(width), full_rows(width)
    loads = [
        pltpu.make_async_copy(ref.at[0], rooms.at[i], sems.at[i]) for i, ref in enumerate((inv_ref, low_ref, up_ref))
    ]
    for load in loads:
        load.start()
    stores = []

    def store(at, rows, *refs):
        where = pl.ds(at, rows)
        for ref in refs:
            target = ref.at[where, :] if ref is node_ref else ref
            stores.append(pltpu.make_async_copy(lines.at[where, :], target, out_sems.at[len(stores)]))
            stores[-1].start()

    loads[0].wait()
    inverse = rooms[0]
    put_sym(lines, 0, inverse)
    store(0, ps, sym_ref, node_ref)
    inv_parts = parts_of(inverse)
    loads[1].wait()
    put_full(lines, ps, times(inv_parts, parts_of(rooms[1])))
    store(ps, pf, g_ref, node_ref)
    loads[2].wait()
    up_high, up_low = parts_of(rooms[2])
    most = width // (2 * lanes) * (2 * lanes)
    for begin, end in ((0, most), (most, width)):
        if begin < end:
            product = times(inv_parts, (up_high[:, begin:end], up_low[:, begin:end]))
            for j in range(begin // lanes, end // lanes):
                lines[pl.ds(ps + pf + j * width, width), :] = product[:, j * lanes - begin : (j + 1) * lanes - begin]
            store(ps + pf + begin // lanes * width, (end - begin) // lanes * width, node_ref)
    for copy in stores:
        copy.wait()


def get_node(ref, width):
    ps, pf = sym_rows(width), full_rows(width)
    return get_sym(ref, 0, width), get_full(ref, ps, width), get_full(ref, ps + pf, width)


def put_state(ref, aa, ba, bb):
    ps = sym_rows(aa.shape[0])
    put_sym(ref, 0, aa)
    put_sym(ref, ps, bb)
    put_full(ref, 2 * ps, ba)


def roles_of(length):
    place = place_now(length)
    return place == 0, place == group, place == 2 * group, place == 3 * group


def ready_kernel(length, node, diag_ref, g_ref, high_ref, low_ref):
    width = diag_ref.shape[0]
    ps, pf = sym_rows(width), full_rows(width)
    at_zero, at_low, at_mid, at_high = roles_of(length)

    @pl.when(jnp.logical_or(jnp.logical_or(at_zero, at_low), jnp.logical_or(at_mid, at_high)))
    def _():
        diag_ref[...] = get_sym(node, 0, width)
        g_mat = get_full(node, ps, width)
        g_ref[...] = g_mat

        @pl.when(at_low)
        def _():
            high_ref[...], low_ref[...] = parts_of(get_full(node, ps + pf, width))

        @pl.when(jnp.logical_not(at_low))
        def _():
            high_ref[...], low_ref[...] = parts_of(g_mat)


def mid_kernel(length, node, diag, g_high, g_low, came_root, out, sym_ref):
    width = out.shape[1]
    ps = sym_rows(width)
    _, _, at_mid, _ = roles_of(length)

    @pl.when(jnp.logical_not(at_mid))
    def _():
        sym_ref[...] = node[pl.ds(0, ps), :]

    @pl.when(at_mid)
    def _():
        left = g_high[...], g_low[...]
        cross = -times(left, parts_of(get_sym(came_root, 0, width)))
        own = diag[...] - symmetric_times(left, parts_of(cross))
        put_sym(sym_ref, 0, own)
        out[0] = cross
        out[1] = own


def first_kernel(length, at_m, root_mid, came_node, kept, sh, sl, aa_ref, bb_ref):
    width = kept.shape[1]
    _, _, at_mid, _ = roles_of(length)

    @pl.when(at_mid)
    def _():
        mid_cross, mid = at_m[0], at_m[1]
        kept[0], kept[1] = mid, mid_cross
        set_state(sh, sl, get_sym(root_mid, 0, width), mid_cross, mid)
        passed, own = eliminate(get_node(came_node, width), sh, sl)
        put_sym(aa_ref, 0, own)
        put_sym(bb_ref, 0, mid)
        set_state(sh, sl, own, passed[:, width:].T, mid)


def second_kernel(
    length, diag, g_ref, high, low, came_d, came_g, came_sym, mid_high, _kept, _sh, _sl, _aa, came_bb, kept, sh, sl, aa_ref, bb_ref, own_ref
):
    width = kept.shape[1]
    ps = sym_rows(width)
    at_zero, at_low, at_mid, at_high = roles_of(length)

    @pl.when(at_mid)
    def _():
        own_ref[...] = came_bb[...]

    @pl.when(at_low)
    def _():
        h_parts = high[...], low[...]
        mid_both = jnp.concatenate([get_full(came_g, 0, width), get_sym(came_d, 0, width)], axis=1)
        both = times(h_parts, parts_of(mid_both))
        e_parts = parts_of(both[:, :width] - g_ref[...])
        root = get_sym(came_sym, 0, width)
        cross = times(e_parts, parts_of(root))
        own = diag[...] + symmetric_times(
            beside(parts_of(both[:, width:]), parts_of(cross)), beside(h_parts, e_parts)
        )
        aa_ref[...] = came_sym[...]
        put_sym(bb_ref, 0, own)
        own_ref[...] = bb_ref[...]
        set_state(sh, sl, root, cross, own)
        kept[0], kept[1] = own, cross

    def above(mid, own_diag, own_g):
        cross = -times(own_g, parts_of(mid))
        return cross, own_diag - symmetric_times(own_g, parts_of(cross))

    @pl.when(at_high)
    def _():
        mid = get_sym(mid_high, 0, width)
        cross, own = above(mid, diag[...], (high[...], low[...]))
        aa_ref[...] = mid_high[...]
        put_sym(bb_ref, 0, own)
        own_ref[...] = bb_ref[...]
        set_state(sh, sl, mid, cross, own)
        kept[0], kept[1] = own, cross

    @pl.when(at_zero)
    def _():
        high_g = parts_of(get_full(came_g, 0, width))
        _, own = above(get_sym(came_sym, 0, width), get_sym(came_d, 0, width), high_g)
        zeros = jnp.zeros((width, width), f32)
        put_sym(aa_ref, 0, own)
        bb_ref[...] = jnp.zeros((ps, lanes), f32)
        set_state(sh, sl, own, zeros, zeros)
        put_sym(own_ref, 0, diag[...])
        kept[0], kept[1] = diag[...], zeros


def state_kernel(aa_ref, ba_ref, bb_ref, own_ref, sh, sl, aa_out, bb_out, own_out):
    aa, bb = aa_ref[...], bb_ref[...]
    put_sym(aa_out, 0, aa)
    put_sym(bb_out, 0, bb)
    put_sym(own_out, 0, own_ref[...])
    set_state(sh, sl, aa, ba_ref[...], bb)


def four_for(length, fours, work):
    place = place_now(length)
    served = lax.rem(place, group) == 0
    if len(fours) == 1:
        pl.when(served)(lambda: work(fours[0]))
    else:
        at_mid = place == 2 * group
        pl.when(at_mid)(lambda: work(fours[1]))
        pl.when(jnp.logical_and(served, jnp.logical_not(at_mid)))(lambda: work(fours[0]))


def cross_kernel(length, sh, sl, *refs):
    fours, (low_ref, high_ref, passed_high, passed_low) = refs[:-4], refs[-4:]
    width = sh.shape[0] // 2

    def work(four):
        _, g_mat, h_mat = get_node(four, width)
        passed = -times(parts_of(jnp.concatenate([g_mat, h_mat], axis=1)), (sh[...], sl[...]))
        put_full(low_ref, 0, passed[:, :width])
        put_full(high_ref, 0, passed[:, width:].T)
        passed_high[...], passed_low[...] = parts_of(passed)

    four_for(length, fours, work)


def ends_kernel(length, passed_high, passed_low, aa_ref, bb_ref, cross_ref, *refs):
    fours, (low_ends, high_ends, mid_ref, high_ref) = refs[:-4], refs[-4:]
    ps = mid_ref.shape[0]
    width = passed_high.shape[0]

    def work(four):
        diag, g_mat, h_mat = get_node(four, width)
        left = parts_of(jnp.concatenate([g_mat, h_mat], axis=1))
        put_sym(mid_ref, 0, diag - symmetric_times(left, (passed_high[...], passed_low[...])))
        for ref, at in ((low_ends, ps), (high_ends, 0), (high_ref, 0)):
            ref[pl.ds(at, ps), :] = mid_ref[...]
        low_ends[pl.ds(0, ps), :] = aa_ref[...]
        high_ends[pl.ds(ps, ps), :] = bb_ref[...]
        high_ref[pl.ds(ps, ps), :] = bb_ref[...]
        high_ref[pl.ds(2 * ps, cross_ref.shape[0]), :] = cross_ref[...]

    four_for(length, fours, work)


def offset_of(length):
    return lax.rem(place_now(length), group)


def near_kernel(length, late, node, *refs):
    f_high, f_low, rest_ref = refs[-3:]
    width = rest_ref.shape[0]
    offset = offset_of(length)
    turn = lax.rem(offset, group // 2)
    first, second = slice(0, width), slice(width, 2 * width)

    def put(rows, columns, mat):
        f_high[rows, columns], f_low[rows, columns] = parts_of(mat)

    def odd(below, two):
        d_own, g_own, h_own = get_node(node, width)
        d_two, g_two, h_two = get_node(two, width)
        inward, outward = (h_own, g_own) if below else (g_own, h_own)
        inward = parts_of(inward)
        to_low, to_high = times(inward, parts_of(g_two)), times(inward, parts_of(h_two))
        put(first, first, to_low - outward if below else to_low)
        put(first, second, to_high if below else to_high - outward)
        link = -times(inward, parts_of(d_two))
        rest_ref[:, first] = d_own - times(inward, parts_of(link), True)
        if not below:
            put(second, first, -g_two)
            put(second, second, -h_two)
            rest_ref[:, second] = link

    if late:
        pl.when(offset == group - 1)(lambda: odd(False, refs[0]))
        return
    came_near, came_far = refs[:2]
    pl.when(turn == 1)(lambda: odd(True, came_near))
    pl.when(offset == 3)(lambda: odd(False, came_far))

    @pl.when(turn == 2)
    def _():
        d_own, g_own, h_own = get_node(node, width)
        put(first, first, -g_own)
        put(first, second, -h_own)
        rest_ref[:, first] = d_own


def choose_kernel(length, first, third, fifth, *refs):
    out_ref = refs[-1]
    offset = offset_of(length)
    refs = iter(refs)
    for at, count in ((1, first), (3, third), (5, fifth)):
        parts = [next(refs) for _ in range(count)]

        @pl.when(offset == at)
        def _(parts=parts):
            begin = 0
            for part in parts:
                rows = part.shape[0]
                out_ref[pl.ds(begin, rows), :] = part[...]
                begin += rows


def lower_kernel(length, parity, early, late, seven, fh, fl, rest, kept, *refs):
    diag_ref, cross_ref, diag_out, cross_out, sh, sl, sems = refs[-7:]
    width = rest.shape[0]
    ps = sym_rows(width)
    offset = offset_of(length)
    turn = lax.rem(offset, group // 2)
    first, second = slice(0, width), slice(width, 2 * width)
    diag_copy = pltpu.make_async_copy(diag_out, diag_ref.at[0], sems.at[0])
    cross_copy = pltpu.make_async_copy(cross_out, cross_ref.at[0], sems.at[1])

    def finish():
        diag_copy.start()
        diag_copy.wait()
        cross_copy.wait()

    def load(ends, cross, at=0):
        set_state(sh, sl, get_sym(ends, 0, width), get_full(cross, at, width), get_sym(ends, ps, width))

    pl.when(jnp.logical_and(turn == (1 if parity else 2), offset < 3))(lambda: load(early, late))
    pl.when(jnp.logical_and(turn == (1 if parity else 2), offset > 4))(lambda: load(late, early))

    def passed_on():
        return times((fh[first, :], fl[first, :]), (sh[...], sl[...]))

    @pl.when(turn == (1 if parity else 2))
    def _():
        passed = passed_on()
        cross_out[...] = passed[:, first]
        cross_copy.start()
        diag_out[...] = rest[:, first] + symmetric_times(parts_of(passed), (fh[first, :], fl[first, :]))
        finish()

    if parity == 0:

        @pl.when(offset == group // 2)
        def _():
            cross_out[...] = get_full(early, 0, width)
            cross_copy.start()
            diag_out[...] = get_sym(late, ps, width)
            finish()

    else:

        pl.when(offset == 3)(lambda: load(late, early))
        pl.when(offset == group - 1)(lambda: load(seven, seven, 2 * ps))

        @pl.when(turn == 3)
        def _():
            left = long_left(parts_of(passed_on()))
            whole = long_times(left, long_right((fh[...], fl[...]), True), True) + rest[...]
            diag_out[...], cross_out[...] = whole[:, first], whole[:, second]
            cross_copy.start()
            finish()

        @pl.when(offset == 0)
        def _():
            diag_out[...], cross_out[...] = kept[0], kept[1]
            cross_copy.start()
            finish()


def sent(array, length, *moves):
    device = lambda position: (position - row_offset) % length
    pairs = [(device(p), device(p + by)) for by, wanted in moves for p in range(length) if wanted(p)]
    return lax.ppermute(array, axis, pairs)


def upper_levels(inverse, lowers, uppers, length):
    width = inverse.shape[0]
    place = (lax.axis_index(axis) + row_offset) % length
    product = functools.partial(jnp.dot, precision=lax.Precision.HIGHEST, preferred_element_type=f32)
    node_g, node_h = product(inverse, lowers), product(inverse, uppers)
    everywhere = lambda p: True
    zeros = jnp.zeros((width, width), f32)
    sigma = jnp.where(place == 0, inverse, zeros)
    low_own, high_own, cross = zeros, zeros, zeros
    stride = length // 2
    while stride >= group:
        from_low, owned_high = (sent(x, length, (stride, everywhere)) for x in (sigma, high_own))
        from_high, owned_low = (sent(x, length, (-stride, everywhere)) for x in (sigma, low_own))
        has_upper = place + stride < length
        sigma_high = jnp.where(has_upper, from_high, zeros)
        sigma_ba = jnp.where(has_upper, owned_high.T + owned_low, zeros)
        active = place % (2 * stride) == stride
        low = -(product(node_g, from_low) + product(node_h, sigma_ba))
        high = -(product(node_g, sigma_ba.T) + product(node_h, sigma_high))
        own = inverse - product(node_g, low.T) - product(node_h, high.T)
        sigma = jnp.where(active, own, sigma)
        low_own = jnp.where(active, low, zeros)
        high_own = jnp.where(active, high, zeros)
        cross = jnp.where(active, low, cross)
        stride //= 2
    newest = lambda p: p % (2 * group) == group
    below_aa, below_ba, below_bb = (sent(x, length, (group, newest)) for x in (sigma, high_own.T, sigma_high))
    return sigma, cross, tuple(
        jnp.where(active, *pair) for pair in ((from_low, below_aa), (low_own, below_ba), (sigma, below_bb))
    )


def body(inv_diag, low_coupling, up_coupling):
    width = inv_diag.shape[1]
    length = lax.axis_size(axis)
    span = 4 * group
    is_open = length == span
    ps, pf = sym_rows(width), full_rows(width)
    node_rows, state_rows = ps + 2 * pf, 2 * ps + pf
    rows_of = lambda rows: jax.ShapeDtypeStruct((rows, lanes), f32)
    square = (width, width)
    whole = jax.ShapeDtypeStruct((1,) + square, f32)
    vmem, anywhere = pl.BlockSpec(memory_space=pltpu.VMEM), pl.BlockSpec(memory_space=pl.ANY)
    room = lambda *shape, kind=f32: pltpu.VMEM(shape, kind)
    sems = pltpu.SemaphoreType.DMA((4,))
    run = lambda kernel, mib, flops=1, **more: pl.pallas_call(
        kernel, compiler_params=pltpu.CompilerParams(vmem_limit_bytes=mib * 2**20),
        cost_estimate=pl.CostEstimate(flops=flops, bytes_accessed=1, transcendentals=0), **more
    )
    at = lambda turn: (lambda p: p % span == turn)
    inner = lambda offset: (lambda p: p % group == offset)
    mid, half = 2 * group, group // 2

    sym, g_only, node = run(
        own_kernel, 60, out_shape=(rows_of(ps), rows_of(pf), rows_of(node_rows)),
        in_specs=[anywhere] * 3, out_specs=[anywhere] * 3,
        scratch_shapes=[room(3, *square), room(node_rows, lanes), sems, pltpu.SemaphoreType.DMA((6,))], name="own",
    )(inv_diag, low_coupling, up_coupling)

    close = ((-1, inner(2)), (-1, inner(6)))
    away = ((1, inner(2)), (group // 2, inner(6)))
    half_state = (jax.ShapeDtypeStruct((2 * width, 2 * width), bf16),) * 2 + (rows_of(ps),) * 2
    if is_open:
        to_mid = lambda p: p == mid - half
        came_far = sent(
            node, length, (half, lambda p: inner(half)(p) and not to_mid(p)), (group, at(group)), *away
        )
        came_near = sent(node, length, (half, to_mid), *close)
        came_g = sent(g_only, length, (-group, at(mid)), (group, at(3 * group)))
        came_d = sent(sym, length, (mid, at(0)), (-group, at(mid)), (group, at(3 * group)))
        two = jax.ShapeDtypeStruct((2,) + square, f32)
        one = jax.ShapeDtypeStruct(square, f32)
        ready = run(
            functools.partial(ready_kernel, length), 16,
            out_shape=(one, one) + (jax.ShapeDtypeStruct(square, bf16),) * 2,
            in_specs=[vmem], out_specs=[vmem] * 4, name="ready",
        )(node)
        at_m, mid_sym = run(
            functools.partial(mid_kernel, length), 16, 4 * 10**9, out_shape=(two, rows_of(ps)),
            in_specs=[vmem] * 5, out_specs=[vmem] * 2, name="middle",
        )(node, ready[0], *ready[2:], came_d)
        came_sym = sent(mid_sym, length, (mid, at(mid)), (group, at(0)))
        mid_high = sent(mid_sym, length, (group, at(mid)))
        made = run(
            functools.partial(first_kernel, length), 16, out_shape=(two,) + half_state,
            in_specs=[vmem] * 3, out_specs=[vmem] * 5, name="first",
        )(at_m, came_d, came_far)
        kept, *ends, ended = run(
            functools.partial(second_kernel, length), 16, 5 * 10**9, out_shape=(two,) + half_state + (rows_of(ps),),
            in_specs=[vmem] * 13, out_specs=[vmem] * 6,
            input_output_aliases={8 + i: i for i in range(5)}, name="second",
        )(*ready, came_d, came_g, came_sym, mid_high, *made)
        fours = (came_far, came_near)
    else:
        came_far = sent(node, length, (half, inner(half)), *away)
        came_near = sent(node, length, *close)
        diag, cross, below = upper_levels(inv_diag[0], low_coupling[0], up_coupling[0], length)
        kept = jnp.stack([diag, cross])
        *ends, ended = run(
            state_kernel, 16, out_shape=half_state + (rows_of(ps),), in_specs=[vmem] * 4, out_specs=[vmem] * 5,
            name="state",
        )(*below, diag)
        fours = (came_far,)
    one_end = sent(ended, length, (1, inner(0)))
    served = len(fours)
    low_cross, high_cross, *passed = run(
        functools.partial(cross_kernel, length), 16,
        out_shape=(rows_of(pf),) * 2 + (jax.ShapeDtypeStruct((width, 2 * width), bf16),) * 2,
        in_specs=[vmem] * (2 + served), out_specs=[vmem] * 4, name="halve",
    )(*ends[:2], *fours)
    three_cross = sent(low_cross, length, (-5, inner(0)))
    five_cross = sent(high_cross, length, (-3, inner(0)))
    low_ends, high_ends, half_mid, high_half = run(
        functools.partial(ends_kernel, length), 16,
        out_shape=(rows_of(2 * ps),) * 2 + (rows_of(ps), rows_of(state_rows)),
        in_specs=[vmem] * (5 + served), out_specs=[vmem] * 4, name="halves",
    )(*passed, *ends[2:], high_cross, *fours)
    five_ends = sent(high_ends, length, (-3, inner(0)))
    one_mid = sent(half_mid, length, (-7, inner(0)))
    three_ends = sent(low_ends, length, (-5, inner(0)))
    shapes = (jax.ShapeDtypeStruct((2 * width, 2 * width), bf16),) * 2 + (jax.ShapeDtypeStruct((width, 2 * width), f32),)
    composed = run(
        functools.partial(near_kernel, length, False), 16, 4 * 10**9, out_shape=shapes,
        in_specs=[vmem] * 3 + [anywhere], out_specs=[vmem] * 3, name="near",
    )(node, came_near, came_far, one_end)
    by_three, _ = lax.optimization_barrier((three_cross, composed[2]))
    one_cross = sent(by_three, length, (-2, inner(3)))
    to_seven = sent(high_half, length, (-1, inner(0)))
    later, _ = lax.optimization_barrier((came_far, three_cross))
    came_back = sent(later, length, (-3, inner(2)))

    f_high, f_low, rest = run(
        functools.partial(near_kernel, length, True), 16, out_shape=shapes,
        in_specs=[vmem] * 2 + [vmem] * 3, out_specs=[vmem] * 3, name="back",
        input_output_aliases={2: 0, 3: 1, 4: 2},
    )(node, came_back, *composed)

    def chosen(name, flops, *groups, after=()):
        return run(
            functools.partial(choose_kernel, length, *map(len, groups)), 16, flops,
            out_shape=rows_of(2 * ps), in_specs=[vmem] * sum(map(len, groups)) + [anywhere] * len(after),
            out_specs=vmem, name=name,
        )(*(array for arrays in groups for array in arrays), *after)

    early = chosen("early", 1, (one_end, one_mid), (three_cross,), (five_cross,), after=(composed[2],))
    late = chosen("late", 4 * 10**9, (one_cross,), (three_ends,), (five_ends,), after=(early,))
    early_next, late_next = (sent(x, length, (1, inner(1)), (1, inner(3)), (1, inner(5))) for x in (early, late))

    outputs = ()
    for parity, came in ((1, (early, late)), (0, (early_next, late_next))):
        outputs = run(
            functools.partial(lower_kernel, length, parity), 20,
            out_shape=(whole, whole), in_specs=[vmem] * 7 + [anywhere] * len(outputs), out_specs=[anywhere] * 2,
            scratch_shapes=[room(*square)] * 2 + [room(2 * width, 2 * width, kind=bf16)] * 2 + [sems],
            input_output_aliases={7 + i: i for i in range(len(outputs))}, name="lower",
        )(*came, to_seven, f_high, f_low, rest, kept, *outputs)
    return outputs


def solution(mesh):
    placed = (P(axis, None, None),) * 3
    return jax.shard_map(
        body, mesh=mesh, in_specs=placed, out_specs=placed[:2], check_vma=False
    )
```

profile of v0, /device:TPU:3, one launch (start us, length us, event | category | flops | bytes accessed | tf_op | source)
XLA Modules:
  0.0 61.3 jit_solution(10817669788780516636)
XLA Ops:
  0.6 3.7 %own.1 = (f32[648,128]{1,0:T(8,128)}, f32[1152,128]{1,0:T(8,128)}, f32[2952,128]{1,0:T(8,128)}) custom-call(f32[1,384,384]{2,1,0:T(8,128)} %inv_ref.1, f32[1,384,384]{2,1,0:T(8,128)} %low_ref.1, f32[1,384,384]{2,1,0:T(8,128)} %up_ref.1), custom_call_target="tpu_custom_call" | custom-call | flops 1 | bytes 1 | tf_op jit(solution)/shard_map/own/pallas_call | solution.py:557
  4.3 3.2 %collective-permute-start.4 = (f32[2952,128]{1,0:T(8,128)}, f32[2952,128]{1,0:T(8,128)S(1)}, u32[]{:S(2)}, u32[]{:S(2)}) collective-permute-start(f32[2952,128]{1,0:T(8,128)} %get-tuple-element.40.node), channel_id=1, source_target_pairs={{1,5},{17,21},{25,29},{5,13},{31,0},{7,8},{15,16},{23,24},{3,7},{1... | collective-permute-start | bytes 4534280 | tf_op jit(solution)/shard_map/ppermute | solution.py:501
  7.6 0.7 %collective-permute-start = (f32[648,128]{1,0:T(8,128)}, f32[648,128]{1,0:T(8,128)S(1)}, u32[]{:S(2)}, u32[]{:S(2)}) collective-permute-start(f32[648,128]{1,0:T(8,128)} %get-tuple-element.45), channel_id=1, source_target_pairs={{29,13},{13,5},{21,29}} | collective-permute-start | bytes 995336 | tf_op jit(solution)/shard_map/ppermute | solution.py:501
  8.3 1.4 %collective-permute-start.6 = (f32[2952,128]{1,0:T(8,128)}, f32[2952,128]{1,0:T(8,128)S(1)}, u32[]{:S(2)}, u32[]{:S(2)}) collective-permute-start(f32[2952,128]{1,0:T(8,128)} %get-tuple-element.40.node), channel_id=1, source_target_pairs={{9,13},{31,30},{7,6},{15,14},{23,22},{3,2},{11,10},{19,18},{27,26}} | collective-permute-start | bytes 4534280 | tf_op jit(solution)/shard_map/ppermute | solution.py:501
  9.7 0.7 %collective-permute-start.1 = (f32[1152,128]{1,0:T(8,128)}, f32[1152,128]{1,0:T(8,128)S(1)}, u32[]{:S(2)}, u32[]{:S(2)}) collective-permute-start(f32[1152,128]{1,0:T(8,128)} %get-tuple-element.46), channel_id=1, source_target_pairs={{13,5},{21,29}} | collective-permute-start | bytes 1769480 | tf_op jit(solution)/shard_map/ppermute | solution.py:501
  10.4 1.4 %copy-done = f32[2952,128]{1,0:T(8,128)S(1)} copy-done((f32[2952,128]{1,0:T(8,128)S(1)}, f32[2952,128]{1,0:T(8,128)}, u32[]{:S(2)}) %copy-start) | copy-done | bytes 1511448
  11.8 0.0 collective-permute-done.came_root.root_mid.came_d
  11.8 0.7 %collective-permute-start.2 = (f32[648,128]{1,0:T(8,128)S(1)}, f32[648,128]{1,0:T(8,128)S(1)}, u32[]{:S(2)}, u32[]{:S(2)}) collective-permute-start(f32[648,128]{1,0:T(8,128)S(1)} %get-tuple-element.47), channel_id=1, source_target_pairs={{13,29},{29,5}} | collective-permute-start | bytes 995336 | tf_op jit(solution)/shard_map/ppermute | solution.py:501
  12.5 0.7 %collective-permute-start.3 = (f32[648,128]{1,0:T(8,128)S(1)}, f32[648,128]{1,0:T(8,128)S(1)}, u32[]{:S(2)}, u32[]{:S(2)}) collective-permute-start(f32[648,128]{1,0:T(8,128)S(1)} %get-tuple-element.47), channel_id=1, source_target_pairs={{13,21}} | collective-permute-start | bytes 995336 | tf_op jit(solution)/shard_map/ppermute | solution.py:501
  13.2 11.3 %collective-permute-done.4.came_node.refs_0_.refs_1_ = f32[2952,128]{1,0:T(8,128)S(1)} collective-permute-done((f32[2952,128]{1,0:T(8,128)}, f32[2952,128]{1,0:T(8,128)S(1)}, u32[]{:S(2)}, u32[]{:S(2)}) %collective-permute-start.4) | collective-permute-done | bytes 1511456 | tf_op jit(solution)/shard_map/ppermute | solution.py:501
  24.5 0.0 collective-permute-done.1.came_g
  24.5 0.0 collective-permute-done.2.came_sym
  24.5 0.0 collective-permute-done.3.mid_high
  24.5 0.7 %collective-permute-start.5 = (f32[648,128]{1,0:T(8,128)S(1)}, f32[648,128]{1,0:T(8,128)S(1)}, u32[]{:S(2)}, u32[]{:S(2)}) collective-permute-start(f32[648,128]{1,0:T(8,128)S(1)} %get-tuple-element.54), channel_id=1, source_target_pairs={{29,30},{5,6},{13,14},{21,22}} | collective-permute-start | bytes 995336 | tf_op jit(solution)/shard_map/ppermute | solution.py:501
  25.2 0.2 halve.1
  25.5 0.7 %collective-permute-start.8 = (f32[1152,128]{1,0:T(8,128)S(1)}, f32[1152,128]{1,0:T(8,128)S(1)}, u32[]{:S(2)}, u32[]{:S(2)}) collective-permute-start(f32[1152,128]{1,0:T(8,128)S(1)} %get-tuple-element.63), channel_id=1, source_target_pairs={{29,24},{5,0},{13,8},{21,16}} | collective-permute-start | bytes 1769480 | tf_op jit(solution)/shard_map/ppermute | solution.py:501
  26.2 0.7 %collective-permute-start.9 = (f32[1152,128]{1,0:T(8,128)S(1)}, f32[1152,128]{1,0:T(8,128)S(1)}, u32[]{:S(2)}, u32[]{:S(2)}) collective-permute-start(f32[1152,128]{1,0:T(8,128)S(1)} %get-tuple-element.61.cross_ref), channel_id=1, source_target_pairs={{29,26},{5,2},{13,10},{21,18}} | collective-permute-start | bytes 1769480 | tf_op jit(solution)/shard_map/ppermute | solution.py:501
  26.9 0.8 %collective-permute-start.7 = (f32[648,128]{1,0:T(8,128)S(1)}, f32[648,128]{1,0:T(8,128)S(1)}, u32[]{:S(2)}, u32[]{:S(2)}) collective-permute-start(f32[648,128]{1,0:T(8,128)S(1)} %get-tuple-element.62), channel_id=1, source_target_pairs={{29,22},{5,30},{13,6},{21,14}} | collective-permute-start | bytes 995336 | tf_op jit(solution)/shard_map/ppermute | solution.py:501
  27.7 0.7 %collective-permute-start.12 = (f32[1296,128]{1,0:T(8,128)S(1)}, f32[1296,128]{1,0:T(8,128)S(1)}, u32[]{:S(2)}, u32[]{:S(2)}) collective-permute-start(f32[1296,128]{1,0:T(8,128)S(1)} %get-tuple-element.66), channel_id=1, source_target_pairs={{29,24},{5,0},{13,8},{21,16}} | collective-permute-start | bytes 1990664 | tf_op jit(solution)/shard_map/ppermute | solution.py:501
  28.4 0.0 collective-permute-done.5.refs_2_.refs_0_
  28.5 0.7 %collective-permute-start.13 = (f32[1296,128]{1,0:T(8,128)S(1)}, f32[1296,128]{1,0:T(8,128)S(1)}, u32[]{:S(2)}, u32[]{:S(2)}) collective-permute-start(f32[1296,128]{1,0:T(8,128)S(1)} %get-tuple-element.67), channel_id=1, source_target_pairs={{29,26},{5,2},{13,10},{21,18}} | collective-permute-start | bytes 1990664 | tf_op jit(solution)/shard_map/ppermute | solution.py:501
  29.2 0.5 near.1
  29.6 0.7 %collective-permute-start.11 = (f32[1152,128]{1,0:T(8,128)S(1)}, f32[1152,128]{1,0:T(8,128)S(1)}, u32[]{:S(2)}, u32[]{:S(2)}) collective-permute-start(f32[1152,128]{1,0:T(8,128)S(1)} %collective-permute-done.8.refs_2_), channel_id=1, source_target_pairs={{0,30},{8,6},{16,14},{24,22}} | collective-permute-start | bytes 1769480 | tf_op jit(solution)/shard_map/ppermute | solution.py:501
  30.4 0.8 %collective-permute-start.16 = (f32[2952,128]{1,0:T(8,128)S(1)}, f32[2952,128]{1,0:T(8,128)S(1)}, u32[]{:S(2)}, u32[]{:S(2)}) collective-permute-start(f32[2952,128]{1,0:T(8,128)S(1)} %collective-permute-done.4.came_node.refs_0_.refs_1_), channel_id=1, source_target_pairs={{31,28},{7,4},{15,12},{23,20}} | collective-permute-start | bytes 4534280 | tf_op jit(solution)/shard_map/ppermute | solution.py:501
  31.1 0.7 %collective-permute-start.15 = (f32[2448,128]{1,0:T(8,128)S(1)}, f32[2448,128]{1,0:T(8,128)S(1)}, u32[]{:S(2)}, u32[]{:S(2)}) collective-permute-start(f32[2448,128]{1,0:T(8,128)S(1)} %get-tuple-element.68), channel_id=1, source_target_pairs={{29,28},{5,4},{13,12},{21,20}} | collective-permute-start | bytes 3760136 | tf_op jit(solution)/shard_map/ppermute | solution.py:501
  31.9 1.3 %collective-permute-start.10 = (f32[1296,128]{1,0:T(8,128)S(1)}, f32[1296,128]{1,0:T(8,128)S(1)}, u32[]{:S(2)}, u32[]{:S(2)}) collective-permute-start(f32[1296,128]{1,0:T(8,128)S(1)} %early.1.refs_3_), channel_id=1, source_target_pairs={{30,31},{6,7},{14,15},{22,23},{0,1},{8,9},{16,17},{24,25},{2,3},{1... | collective-permute-start | bytes 1990664 | tf_op jit(solution)/shard_map/ppermute | solution.py:501
  33.3 1.3 %collective-permute-start.14 = (f32[1296,128]{1,0:T(8,128)S(1)}, f32[1296,128]{1,0:T(8,128)S(1)}, u32[]{:S(2)}, u32[]{:S(2)}) collective-permute-start(f32[1296,128]{1,0:T(8,128)S(1)} %late.1), channel_id=1, source_target_pairs={{30,31},{6,7},{14,15},{22,23},{0,1},{8,9},{16,17},{24,25},{2,3},{1... | collective-permute-start | bytes 1990664 | tf_op jit(solution)/shard_map/ppermute | solution.py:501
  34.6 0.2 back.1
  34.9 0.1 lower.2
  35.0 15.7 %collective-permute-done.10.early = f32[1296,128]{1,0:T(8,128)S(1)} collective-permute-done((f32[1296,128]{1,0:T(8,128)S(1)}, f32[1296,128]{1,0:T(8,128)S(1)}, u32[]{:S(2)}, u32[]{:S(2)}) %collective-permute-start.10) | collective-permute-done | bytes 663584 | tf_op jit(solution)/shard_map/ppermute | solution.py:501
  50.7 6.3 %collective-permute-done.14.late = f32[1296,128]{1,0:T(8,128)S(1)} collective-permute-done((f32[1296,128]{1,0:T(8,128)S(1)}, f32[1296,128]{1,0:T(8,128)S(1)}, u32[]{:S(2)}, u32[]{:S(2)}) %collective-permute-start.14) | collective-permute-done | bytes 663584 | tf_op jit(solution)/shard_map/ppermute | solution.py:501
  57.0 4.1 %lower.3 = (f32[1,384,384]{2,1,0:T(8,128)}, f32[1,384,384]{2,1,0:T(8,128)}) custom-call(f32[1296,128]{1,0:T(8,128)S(1)} %collective-permute-done.10.early, f32[1296,128]{1,0:T(8,128)S(1)} %collective-permute-done.14.late, f32[2448,128]{1,0:T(8,128)S(1)} %collective-permute-done.15.seven, ...), custom_call_target="tpu_custom_call", output_to_operand_aliasing={{0}: (7, {}), {1}: (8, {})} | custom-call | flops 1 | bytes 1 | tf_op jit(solution)/shard_map/lower/pallas_call | solution.py:654
  (19 shorter events, 0.2 us)
Async XLA Ops:
  4.3 20.2 %collective-permute-start.4 = (f32[2952,128]{1,0:T(8,128)}, f32[2952,128]{1,0:T(8,128)S(1)}, u32[]{:S(2)}, u32[]{:S(2)}) collective-permute-start(f32[2952,128]{1,0:T(8,128)} %get-tuple-element.40.node), channel_id=1, source_target_pairs={{1,5},{17,21},{25,29},{5,13},{31,0},{7,8},{15,16},{23,24},{3,7},{1... | collective-permute-start | bytes 4534280 | tf_op jit(solution)/shard_map/ppermute | solution.py:501
  7.6 4.2 %collective-permute-start = (f32[648,128]{1,0:T(8,128)}, f32[648,128]{1,0:T(8,128)S(1)}, u32[]{:S(2)}, u32[]{:S(2)}) collective-permute-start(f32[648,128]{1,0:T(8,128)} %get-tuple-element.45), channel_id=1, source_target_pairs={{29,13},{13,5},{21,29}} | collective-permute-start | bytes 995336 | tf_op jit(solution)/shard_map/ppermute | solution.py:501
  8.3 17.0 %collective-permute-start.6 = (f32[2952,128]{1,0:T(8,128)}, f32[2952,128]{1,0:T(8,128)S(1)}, u32[]{:S(2)}, u32[]{:S(2)}) collective-permute-start(f32[2952,128]{1,0:T(8,128)} %get-tuple-element.40.node), channel_id=1, source_target_pairs={{9,13},{31,30},{7,6},{15,14},{23,22},{3,2},{11,10},{19,18},{27,26}} | collective-permute-start | bytes 4534280 | tf_op jit(solution)/shard_map/ppermute | solution.py:501
  9.7 14.8 %collective-permute-start.1 = (f32[1152,128]{1,0:T(8,128)}, f32[1152,128]{1,0:T(8,128)S(1)}, u32[]{:S(2)}, u32[]{:S(2)}) collective-permute-start(f32[1152,128]{1,0:T(8,128)} %get-tuple-element.46), channel_id=1, source_target_pairs={{13,5},{21,29}} | collective-permute-start | bytes 1769480 | tf_op jit(solution)/shard_map/ppermute | solution.py:501
  10.4 1.4 %copy-start = (f32[2952,128]{1,0:T(8,128)S(1)}, f32[2952,128]{1,0:T(8,128)}, u32[]{:S(2)}) copy-start(f32[2952,128]{1,0:T(8,128)} %get-tuple-element.40.node) | copy-start | bytes 4534276
  11.8 12.7 %collective-permute-start.2 = (f32[648,128]{1,0:T(8,128)S(1)}, f32[648,128]{1,0:T(8,128)S(1)}, u32[]{:S(2)}, u32[]{:S(2)}) collective-permute-start(f32[648,128]{1,0:T(8,128)S(1)} %get-tuple-element.47), channel_id=1, source_target_pairs={{13,29},{29,5}} | collective-permute-start | bytes 995336 | tf_op jit(solution)/shard_map/ppermute | solution.py:501
  12.5 12.0 %collective-permute-start.3 = (f32[648,128]{1,0:T(8,128)S(1)}, f32[648,128]{1,0:T(8,128)S(1)}, u32[]{:S(2)}, u32[]{:S(2)}) collective-permute-start(f32[648,128]{1,0:T(8,128)S(1)} %get-tuple-element.47), channel_id=1, source_target_pairs={{13,21}} | collective-permute-start | bytes 995336 | tf_op jit(solution)/shard_map/ppermute | solution.py:501
  24.5 3.9 %collective-permute-start.5 = (f32[648,128]{1,0:T(8,128)S(1)}, f32[648,128]{1,0:T(8,128)S(1)}, u32[]{:S(2)}, u32[]{:S(2)}) collective-permute-start(f32[648,128]{1,0:T(8,128)S(1)} %get-tuple-element.54), channel_id=1, source_target_pairs={{29,30},{5,6},{13,14},{21,22}} | collective-permute-start | bytes 995336 | tf_op jit(solution)/shard_map/ppermute | solution.py:501
  25.5 4.2 %collective-permute-start.8 = (f32[1152,128]{1,0:T(8,128)S(1)}, f32[1152,128]{1,0:T(8,128)S(1)}, u32[]{:S(2)}, u32[]{:S(2)}) collective-permute-start(f32[1152,128]{1,0:T(8,128)S(1)} %get-tuple-element.63), channel_id=1, source_target_pairs={{29,24},{5,0},{13,8},{21,16}} | collective-permute-start | bytes 1769480 | tf_op jit(solution)/shard_map/ppermute | solution.py:501
  26.2 5.0 %collective-permute-start.9 = (f32[1152,128]{1,0:T(8,128)S(1)}, f32[1152,128]{1,0:T(8,128)S(1)}, u32[]{:S(2)}, u32[]{:S(2)}) collective-permute-start(f32[1152,128]{1,0:T(8,128)S(1)} %get-tuple-element.61.cross_ref), channel_id=1, source_target_pairs={{29,26},{5,2},{13,10},{21,18}} | collective-permute-start | bytes 1769480 | tf_op jit(solution)/shard_map/ppermute | solution.py:501
  26.9 2.3 %copy-start.1 = (f32[2952,128]{1,0:T(8,128)S(1)}, f32[2952,128]{1,0:T(8,128)}, u32[]{:S(2)}) copy-start(f32[2952,128]{1,0:T(8,128)} %get-tuple-element.40.node) | copy-start | bytes 4534276
  26.9 3.4 %collective-permute-start.7 = (f32[648,128]{1,0:T(8,128)S(1)}, f32[648,128]{1,0:T(8,128)S(1)}, u32[]{:S(2)}, u32[]{:S(2)}) collective-permute-start(f32[648,128]{1,0:T(8,128)S(1)} %get-tuple-element.62), channel_id=1, source_target_pairs={{29,22},{5,30},{13,6},{21,14}} | collective-permute-start | bytes 995336 | tf_op jit(solution)/shard_map/ppermute | solution.py:501
  27.7 4.2 %collective-permute-start.12 = (f32[1296,128]{1,0:T(8,128)S(1)}, f32[1296,128]{1,0:T(8,128)S(1)}, u32[]{:S(2)}, u32[]{:S(2)}) collective-permute-start(f32[1296,128]{1,0:T(8,128)S(1)} %get-tuple-element.66), channel_id=1, source_target_pairs={{29,24},{5,0},{13,8},{21,16}} | collective-permute-start | bytes 1990664 | tf_op jit(solution)/shard_map/ppermute | solution.py:501
  28.5 4.8 %collective-permute-start.13 = (f32[1296,128]{1,0:T(8,128)S(1)}, f32[1296,128]{1,0:T(8,128)S(1)}, u32[]{:S(2)}, u32[]{:S(2)}) collective-permute-start(f32[1296,128]{1,0:T(8,128)S(1)} %get-tuple-element.67), channel_id=1, source_target_pairs={{29,26},{5,2},{13,10},{21,18}} | collective-permute-start | bytes 1990664 | tf_op jit(solution)/shard_map/ppermute | solution.py:501
  29.6 3.6 %collective-permute-start.11 = (f32[1152,128]{1,0:T(8,128)S(1)}, f32[1152,128]{1,0:T(8,128)S(1)}, u32[]{:S(2)}, u32[]{:S(2)}) collective-permute-start(f32[1152,128]{1,0:T(8,128)S(1)} %collective-permute-done.8.refs_2_), channel_id=1, source_target_pairs={{0,30},{8,6},{16,14},{24,22}} | collective-permute-start | bytes 1769480 | tf_op jit(solution)/shard_map/ppermute | solution.py:501
  30.4 4.2 %collective-permute-start.16 = (f32[2952,128]{1,0:T(8,128)S(1)}, f32[2952,128]{1,0:T(8,128)S(1)}, u32[]{:S(2)}, u32[]{:S(2)}) collective-permute-start(f32[2952,128]{1,0:T(8,128)S(1)} %collective-permute-done.4.came_node.refs_0_.refs_1_), channel_id=1, source_target_pairs={{31,28},{7,4},{15,12},{23,20}} | collective-permute-start | bytes 4534280 | tf_op jit(solution)/shard_map/ppermute | solution.py:501
  31.1 3.7 %collective-permute-start.15 = (f32[2448,128]{1,0:T(8,128)S(1)}, f32[2448,128]{1,0:T(8,128)S(1)}, u32[]{:S(2)}, u32[]{:S(2)}) collective-permute-start(f32[2448,128]{1,0:T(8,128)S(1)} %get-tuple-element.68), channel_id=1, source_target_pairs={{29,28},{5,4},{13,12},{21,20}} | collective-permute-start | bytes 3760136 | tf_op jit(solution)/shard_map/ppermute | solution.py:501
  31.9 18.8 %collective-permute-start.10 = (f32[1296,128]{1,0:T(8,128)S(1)}, f32[1296,128]{1,0:T(8,128)S(1)}, u32[]{:S(2)}, u32[]{:S(2)}) collective-permute-start(f32[1296,128]{1,0:T(8,128)S(1)} %early.1.refs_3_), channel_id=1, source_target_pairs={{30,31},{6,7},{14,15},{22,23},{0,1},{8,9},{16,17},{24,25},{2,3},{1... | collective-permute-start | bytes 1990664 | tf_op jit(solution)/shard_map/ppermute | solution.py:501
  33.3 23.8 %collective-permute-start.14 = (f32[1296,128]{1,0:T(8,128)S(1)}, f32[1296,128]{1,0:T(8,128)S(1)}, u32[]{:S(2)}, u32[]{:S(2)}) collective-permute-start(f32[1296,128]{1,0:T(8,128)S(1)} %late.1), channel_id=1, source_target_pairs={{30,31},{6,7},{14,15},{22,23},{0,1},{8,9},{16,17},{24,25},{2,3},{1... | collective-permute-start | bytes 1990664 | tf_op jit(solution)/shard_map/ppermute | solution.py:501
where the time goes:
time: 62.1 us; the launch traced here: 61.3 us
  waiting for transfers between devices  33.4 us (54%)
  starting transfers between devices  16.5 us (27%)
  Pallas kernels  8.88 us (14%)
  local copies, waits for them, and re-layouts  1.38 us (2%)
  between operations  1.13 us (2%)
    ppermute x17, waiting for transfers between devices, sent(): return lax.ppermute(array, axis, pairs)  33.4 us
    ppermute x17, starting transfers between devices, sent(): return lax.ppermute(array, axis, pairs)  16.5 us
    pallas_call x2, Pallas kernels, body(): run(functools.partial(lower_kernel, length, parity), 20, out_shape=(whole...  4.14 us
    pallas_call x1, Pallas kernels, body(): run(own_kernel, 60, out_shape=(rows_of(ps), rows_of(pf), rows_of(node_row...  3.7 us
    unnamed x4, local copies, waits for them, and re-layouts  1.38 us
  transfers between devices with their start and end apart: 17, of which 3 were waited for; matrix products, arithmetic and copies ran while one was open for 0% of the time, Pallas kernels for 2%

commit v1 on v0

--- a/solution.py
+++ b/solution.py
@@ -269,7 +269,7 @@
 
 
 def second_kernel(
-    length, diag, g_ref, high, low, came_d, came_g, came_sym, mid_high, _kept, _sh, _sl, _aa, came_bb, kept, sh, sl, aa_ref, bb_ref, own_ref
+    length, diag, g_ref, high, low, came_d, came_g, came_sym, mid_high, came_kept, came_sh, came_sl, came_aa, came_bb, kept, sh, sl, aa_ref, bb_ref, own_ref
 ):
     width = kept.shape[1]
     ps = sym_rows(width)
@@ -278,6 +278,8 @@
     @pl.when(at_mid)
     def _():
         own_ref[...] = came_bb[...]
+        for ref, came in ((kept, came_kept), (sh, came_sh), (sl, came_sl), (aa_ref, came_aa), (bb_ref, came_bb)):
+            ref[...] = came[...]
 
     @pl.when(at_low)
     def _():
@@ -405,6 +407,12 @@
 
     if late:
         pl.when(offset == group - 1)(lambda: odd(False, refs[0]))
+
+        @pl.when(offset != group - 1)
+        def _():
+            for ref, came in zip(refs[-3:], refs[1:4]):
+                ref[...] = came[...]
+
         return
     came_near, came_far = refs[:2]
     pl.when(turn == 1)(lambda: odd(True, came_near))

time: 62.1 us -> 62.1 us (level)
  transfers between devices with their start and end apart: 17 -> 17, of which waited for: 3 -> 3; matrix products, arithmetic and copies ran while one was open for 0% -> 0% of each run, Pallas kernels for 2% -> 3%
where the time goes in v1:
time: 62.1 us; the launch traced here: 61.3 us
  waiting for transfers between devices  33 us (53%)
  starting transfers between devices  16.5 us (27%)
  Pallas kernels  9.31 us (15%)
  local copies, waits for them, and re-layouts  1.38 us (2%)
  between operations  1.13 us (2%)
    ppermute x17, waiting for transfers between devices, sent(): return lax.ppermute(array, axis, pairs)  33 us
    ppermute x17, starting transfers between devices, sent(): return lax.ppermute(array, axis, pairs)  16.5 us
    pallas_call x2, Pallas kernels, body(): run(functools.partial(lower_kernel, length, parity), 20, out_shape=(whole...  4.14 us
    pallas_call x1, Pallas kernels, body(): run(own_kernel, 60, out_shape=(rows_of(ps), rows_of(pf), rows_of(node_row...  3.7 us
    unnamed x4, local copies, waits for them, and re-layouts  1.38 us
  transfers between devices with their start and end apart: 17, of which 3 were waited for; matrix products, arithmetic and copies ran while one was open for 0% of the time, Pallas kernels for 3%

profile of v1, /device:TPU:3, one launch (start us, length us, event | category | flops | bytes accessed | tf_op | source)
XLA Modules:
  0.0 61.3 jit_solution(3599727151888112652)
XLA Ops:
  0.6 3.7 %own.1 = (f32[648,128]{1,0:T(8,128)}, f32[1152,128]{1,0:T(8,128)}, f32[2952,128]{1,0:T(8,128)}) custom-call(f32[1,384,384]{2,1,0:T(8,128)} %inv_ref.1, f32[1,384,384]{2,1,0:T(8,128)} %low_ref.1, f32[1,384,384]{2,1,0:T(8,128)} %up_ref.1), custom_call_target="tpu_custom_call" | custom-call | flops 1 | bytes 1 | tf_op jit(solution)/shard_map/own/pallas_call | solution.py:565
  4.3 3.2 %collective-permute-start.4 = (f32[2952,128]{1,0:T(8,128)}, f32[2952,128]{1,0:T(8,128)S(1)}, u32[]{:S(2)}, u32[]{:S(2)}) collective-permute-start(f32[2952,128]{1,0:T(8,128)} %get-tuple-element.40.node), channel_id=1, source_target_pairs={{1,5},{17,21},{25,29},{5,13},{31,0},{7,8},{15,16},{23,24},{3,7},{1... | collective-permute-start | bytes 4534280 | tf_op jit(solution)/shard_map/ppermute | solution.py:509
  7.6 0.7 %collective-permute-start = (f32[648,128]{1,0:T(8,128)}, f32[648,128]{1,0:T(8,128)S(1)}, u32[]{:S(2)}, u32[]{:S(2)}) collective-permute-start(f32[648,128]{1,0:T(8,128)} %get-tuple-element.45), channel_id=1, source_target_pairs={{29,13},{13,5},{21,29}} | collective-permute-start | bytes 995336 | tf_op jit(solution)/shard_map/ppermute | solution.py:509
  8.3 1.4 %collective-permute-start.6 = (f32[2952,128]{1,0:T(8,128)}, f32[2952,128]{1,0:T(8,128)S(1)}, u32[]{:S(2)}, u32[]{:S(2)}) collective-permute-start(f32[2952,128]{1,0:T(8,128)} %get-tuple-element.40.node), channel_id=1, source_target_pairs={{9,13},{31,30},{7,6},{15,14},{23,22},{3,2},{11,10},{19,18},{27,26}} | collective-permute-start | bytes 4534280 | tf_op jit(solution)/shard_map/ppermute | solution.py:509
  9.7 0.7 %collective-permute-start.1 = (f32[1152,128]{1,0:T(8,128)}, f32[1152,128]{1,0:T(8,128)S(1)}, u32[]{:S(2)}, u32[]{:S(2)}) collective-permute-start(f32[1152,128]{1,0:T(8,128)} %get-tuple-element.46), channel_id=1, source_target_pairs={{13,5},{21,29}} | collective-permute-start | bytes 1769480 | tf_op jit(solution)/shard_map/ppermute | solution.py:509
  10.4 1.4 %copy-done = f32[2952,128]{1,0:T(8,128)S(1)} copy-done((f32[2952,128]{1,0:T(8,128)S(1)}, f32[2952,128]{1,0:T(8,128)}, u32[]{:S(2)}) %copy-start) | copy-done | bytes 1511448
  11.8 0.0 collective-permute-done.came_root.root_mid.came_d
  11.8 0.7 %collective-permute-start.2 = (f32[648,128]{1,0:T(8,128)S(1)}, f32[648,128]{1,0:T(8,128)S(1)}, u32[]{:S(2)}, u32[]{:S(2)}) collective-permute-start(f32[648,128]{1,0:T(8,128)S(1)} %get-tuple-element.47), channel_id=1, source_target_pairs={{13,29},{29,5}} | collective-permute-start | bytes 995336 | tf_op jit(solution)/shard_map/ppermute | solution.py:509
  12.5 0.7 %collective-permute-start.3 = (f32[648,128]{1,0:T(8,128)S(1)}, f32[648,128]{1,0:T(8,128)S(1)}, u32[]{:S(2)}, u32[]{:S(2)}) collective-permute-start(f32[648,128]{1,0:T(8,128)S(1)} %get-tuple-element.47), channel_id=1, source_target_pairs={{13,21}} | collective-permute-start | bytes 995336 | tf_op jit(solution)/shard_map/ppermute | solution.py:509
  13.2 11.3 %collective-permute-done.4.came_node.refs_0_.refs_1_ = f32[2952,128]{1,0:T(8,128)S(1)} collective-permute-done((f32[2952,128]{1,0:T(8,128)}, f32[2952,128]{1,0:T(8,128)S(1)}, u32[]{:S(2)}, u32[]{:S(2)}) %collective-permute-start.4) | collective-permute-done | bytes 1511456 | tf_op jit(solution)/shard_map/ppermute | solution.py:509
  24.5 0.0 collective-permute-done.1.came_g
  24.5 0.0 collective-permute-done.2.came_sym
  24.5 0.0 collective-permute-done.3.mid_high
  24.5 0.7 %collective-permute-start.5 = (f32[648,128]{1,0:T(8,128)S(1)}, f32[648,128]{1,0:T(8,128)S(1)}, u32[]{:S(2)}, u32[]{:S(2)}) collective-permute-start(f32[648,128]{1,0:T(8,128)S(1)} %get-tuple-element.54), channel_id=1, source_target_pairs={{29,30},{5,6},{13,14},{21,22}} | collective-permute-start | bytes 995336 | tf_op jit(solution)/shard_map/ppermute | solution.py:509
  25.2 0.2 halve.1
  25.5 0.7 %collective-permute-start.8 = (f32[1152,128]{1,0:T(8,128)S(1)}, f32[1152,128]{1,0:T(8,128)S(1)}, u32[]{:S(2)}, u32[]{:S(2)}) collective-permute-start(f32[1152,128]{1,0:T(8,128)S(1)} %get-tuple-element.63), channel_id=1, source_target_pairs={{29,24},{5,0},{13,8},{21,16}} | collective-permute-start | bytes 1769480 | tf_op jit(solution)/shard_map/ppermute | solution.py:509
  26.2 0.7 %collective-permute-start.9 = (f32[1152,128]{1,0:T(8,128)S(1)}, f32[1152,128]{1,0:T(8,128)S(1)}, u32[]{:S(2)}, u32[]{:S(2)}) collective-permute-start(f32[1152,128]{1,0:T(8,128)S(1)} %get-tuple-element.61.cross_ref), channel_id=1, source_target_pairs={{29,26},{5,2},{13,10},{21,18}} | collective-permute-start | bytes 1769480 | tf_op jit(solution)/shard_map/ppermute | solution.py:509
  26.9 0.8 %collective-permute-start.7 = (f32[648,128]{1,0:T(8,128)S(1)}, f32[648,128]{1,0:T(8,128)S(1)}, u32[]{:S(2)}, u32[]{:S(2)}) collective-permute-start(f32[648,128]{1,0:T(8,128)S(1)} %get-tuple-element.62), channel_id=1, source_target_pairs={{29,22},{5,30},{13,6},{21,14}} | collective-permute-start | bytes 995336 | tf_op jit(solution)/shard_map/ppermute | solution.py:509
  27.7 0.7 %collective-permute-start.12 = (f32[1296,128]{1,0:T(8,128)S(1)}, f32[1296,128]{1,0:T(8,128)S(1)}, u32[]{:S(2)}, u32[]{:S(2)}) collective-permute-start(f32[1296,128]{1,0:T(8,128)S(1)} %get-tuple-element.66), channel_id=1, source_target_pairs={{29,24},{5,0},{13,8},{21,16}} | collective-permute-start | bytes 1990664 | tf_op jit(solution)/shard_map/ppermute | solution.py:509
  28.4 0.0 collective-permute-done.5.refs_2_.refs_0_
  28.5 0.7 %collective-permute-start.13 = (f32[1296,128]{1,0:T(8,128)S(1)}, f32[1296,128]{1,0:T(8,128)S(1)}, u32[]{:S(2)}, u32[]{:S(2)}) collective-permute-start(f32[1296,128]{1,0:T(8,128)S(1)} %get-tuple-element.67), channel_id=1, source_target_pairs={{29,26},{5,2},{13,10},{21,18}} | collective-permute-start | bytes 1990664 | tf_op jit(solution)/shard_map/ppermute | solution.py:509
  29.2 0.5 near.1
  29.6 0.7 %collective-permute-start.11 = (f32[1152,128]{1,0:T(8,128)S(1)}, f32[1152,128]{1,0:T(8,128)S(1)}, u32[]{:S(2)}, u32[]{:S(2)}) collective-permute-start(f32[1152,128]{1,0:T(8,128)S(1)} %collective-permute-done.8.refs_2_), channel_id=1, source_target_pairs={{0,30},{8,6},{16,14},{24,22}} | collective-permute-start | bytes 1769480 | tf_op jit(solution)/shard_map/ppermute | solution.py:509
  30.4 0.8 %collective-permute-start.16 = (f32[2952,128]{1,0:T(8,128)S(1)}, f32[2952,128]{1,0:T(8,128)S(1)}, u32[]{:S(2)}, u32[]{:S(2)}) collective-permute-start(f32[2952,128]{1,0:T(8,128)S(1)} %collective-permute-done.4.came_node.refs_0_.refs_1_), channel_id=1, source_target_pairs={{31,28},{7,4},{15,12},{23,20}} | collective-permute-start | bytes 4534280 | tf_op jit(solution)/shard_map/ppermute | solution.py:509
  31.1 0.7 %collective-permute-start.15 = (f32[2448,128]{1,0:T(8,128)S(1)}, f32[2448,128]{1,0:T(8,128)S(1)}, u32[]{:S(2)}, u32[]{:S(2)}) collective-permute-start(f32[2448,128]{1,0:T(8,128)S(1)} %get-tuple-element.68), channel_id=1, source_target_pairs={{29,28},{5,4},{13,12},{21,20}} | collective-permute-start | bytes 3760136 | tf_op jit(solution)/shard_map/ppermute | solution.py:509
  31.9 1.3 %collective-permute-start.10 = (f32[1296,128]{1,0:T(8,128)S(1)}, f32[1296,128]{1,0:T(8,128)S(1)}, u32[]{:S(2)}, u32[]{:S(2)}) collective-permute-start(f32[1296,128]{1,0:T(8,128)S(1)} %early.1.refs_3_), channel_id=1, source_target_pairs={{30,31},{6,7},{14,15},{22,23},{0,1},{8,9},{16,17},{24,25},{2,3},{1... | collective-permute-start | bytes 1990664 | tf_op jit(solution)/shard_map/ppermute | solution.py:509
  33.3 1.3 %collective-permute-start.14 = (f32[1296,128]{1,0:T(8,128)S(1)}, f32[1296,128]{1,0:T(8,128)S(1)}, u32[]{:S(2)}, u32[]{:S(2)}) collective-permute-start(f32[1296,128]{1,0:T(8,128)S(1)} %late.1), channel_id=1, source_target_pairs={{30,31},{6,7},{14,15},{22,23},{0,1},{8,9},{16,17},{24,25},{2,3},{1... | collective-permute-start | bytes 1990664 | tf_op jit(solution)/shard_map/ppermute | solution.py:509
  34.6 0.7 %back.1 = (bf16[768,768]{1,0:T(8,128)(2,1)S(1)}, bf16[768,768]{1,0:T(8,128)(2,1)S(1)}, f32[384,768]{1,0:T(8,128)S(1)}) custom-call(f32[2952,128]{1,0:T(8,128)S(1)} %copy-done.1, f32[2952,128]{1,0:T(8,128)S(1)} %collective-permute-done.16.refs_0_, ...), custom_call_target="tpu_custom_call", output_to_operand_aliasing={{0}: (2, {}), {1}: (3, {}), {2}: (4, {})} | custom-call | flops 1 | bytes 1 | tf_op jit(solution)/shard_map/back/pallas_call | solution.py:643
  35.3 0.1 lower.2
  35.4 15.3 %collective-permute-done.10.early = f32[1296,128]{1,0:T(8,128)S(1)} collective-permute-done((f32[1296,128]{1,0:T(8,128)S(1)}, f32[1296,128]{1,0:T(8,128)S(1)}, u32[]{:S(2)}, u32[]{:S(2)}) %collective-permute-start.10) | collective-permute-done | bytes 663584 | tf_op jit(solution)/shard_map/ppermute | solution.py:509
  50.7 6.3 %collective-permute-done.14.late = f32[1296,128]{1,0:T(8,128)S(1)} collective-permute-done((f32[1296,128]{1,0:T(8,128)S(1)}, f32[1296,128]{1,0:T(8,128)S(1)}, u32[]{:S(2)}, u32[]{:S(2)}) %collective-permute-start.14) | collective-permute-done | bytes 663584 | tf_op jit(solution)/shard_map/ppermute | solution.py:509
  57.0 4.1 %lower.3 = (f32[1,384,384]{2,1,0:T(8,128)}, f32[1,384,384]{2,1,0:T(8,128)}) custom-call(f32[1296,128]{1,0:T(8,128)S(1)} %collective-permute-done.10.early, f32[1296,128]{1,0:T(8,128)S(1)} %collective-permute-done.14.late, f32[2448,128]{1,0:T(8,128)S(1)} %collective-permute-done.15.seven, ...), custom_call_target="tpu_custom_call", output_to_operand_aliasing={{0}: (7, {}), {1}: (8, {})} | custom-call | flops 1 | bytes 1 | tf_op jit(solution)/shard_map/lower/pallas_call | solution.py:662
  (19 shorter events, 0.2 us)
Async XLA Ops:
  4.3 20.2 %collective-permute-start.4 = (f32[2952,128]{1,0:T(8,128)}, f32[2952,128]{1,0:T(8,128)S(1)}, u32[]{:S(2)}, u32[]{:S(2)}) collective-permute-start(f32[2952,128]{1,0:T(8,128)} %get-tuple-element.40.node), channel_id=1, source_target_pairs={{1,5},{17,21},{25,29},{5,13},{31,0},{7,8},{15,16},{23,24},{3,7},{1... | collective-permute-start | bytes 4534280 | tf_op jit(solution)/shard_map/ppermute | solution.py:509
  7.6 4.2 %collective-permute-start = (f32[648,128]{1,0:T(8,128)}, f32[648,128]{1,0:T(8,128)S(1)}, u32[]{:S(2)}, u32[]{:S(2)}) collective-permute-start(f32[648,128]{1,0:T(8,128)} %get-tuple-element.45), channel_id=1, source_target_pairs={{29,13},{13,5},{21,29}} | collective-permute-start | bytes 995336 | tf_op jit(solution)/shard_map/ppermute | solution.py:509
  8.3 17.0 %collective-permute-start.6 = (f32[2952,128]{1,0:T(8,128)}, f32[2952,128]{1,0:T(8,128)S(1)}, u32[]{:S(2)}, u32[]{:S(2)}) collective-permute-start(f32[2952,128]{1,0:T(8,128)} %get-tuple-element.40.node), channel_id=1, source_target_pairs={{9,13},{31,30},{7,6},{15,14},{23,22},{3,2},{11,10},{19,18},{27,26}} | collective-permute-start | bytes 4534280 | tf_op jit(solution)/shard_map/ppermute | solution.py:509
  9.7 14.8 %collective-permute-start.1 = (f32[1152,128]{1,0:T(8,128)}, f32[1152,128]{1,0:T(8,128)S(1)}, u32[]{:S(2)}, u32[]{:S(2)}) collective-permute-start(f32[1152,128]{1,0:T(8,128)} %get-tuple-element.46), channel_id=1, source_target_pairs={{13,5},{21,29}} | collective-permute-start | bytes 1769480 | tf_op jit(solution)/shard_map/ppermute | solution.py:509
  10.4 1.4 %copy-start = (f32[2952,128]{1,0:T(8,128)S(1)}, f32[2952,128]{1,0:T(8,128)}, u32[]{:S(2)}) copy-start(f32[2952,128]{1,0:T(8,128)} %get-tuple-element.40.node) | copy-start | bytes 4534276
  11.8 12.7 %collective-permute-start.2 = (f32[648,128]{1,0:T(8,128)S(1)}, f32[648,128]{1,0:T(8,128)S(1)}, u32[]{:S(2)}, u32[]{:S(2)}) collective-permute-start(f32[648,128]{1,0:T(8,128)S(1)} %get-tuple-element.47), channel_id=1, source_target_pairs={{13,29},{29,5}} | collective-permute-start | bytes 995336 | tf_op jit(solution)/shard_map/ppermute | solution.py:509
  12.5 12.0 %collective-permute-start.3 = (f32[648,128]{1,0:T(8,128)S(1)}, f32[648,128]{1,0:T(8,128)S(1)}, u32[]{:S(2)}, u32[]{:S(2)}) collective-permute-start(f32[648,128]{1,0:T(8,128)S(1)} %get-tuple-element.47), channel_id=1, source_target_pairs={{13,21}} | collective-permute-start | bytes 995336 | tf_op jit(solution)/shard_map/ppermute | solution.py:509
  24.5 3.9 %collective-permute-start.5 = (f32[648,128]{1,0:T(8,128)S(1)}, f32[648,128]{1,0:T(8,128)S(1)}, u32[]{:S(2)}, u32[]{:S(2)}) collective-permute-start(f32[648,128]{1,0:T(8,128)S(1)} %get-tuple-element.54), channel_id=1, source_target_pairs={{29,30},{5,6},{13,14},{21,22}} | collective-permute-start | bytes 995336 | tf_op jit(solution)/shard_map/ppermute | solution.py:509
  25.5 4.2 %collective-permute-start.8 = (f32[1152,128]{1,0:T(8,128)S(1)}, f32[1152,128]{1,0:T(8,128)S(1)}, u32[]{:S(2)}, u32[]{:S(2)}) collective-permute-start(f32[1152,128]{1,0:T(8,128)S(1)} %get-tuple-element.63), channel_id=1, source_target_pairs={{29,24},{5,0},{13,8},{21,16}} | collective-permute-start | bytes 1769480 | tf_op jit(solution)/shard_map/ppermute | solution.py:509
  26.2 5.0 %collective-permute-start.9 = (f32[1152,128]{1,0:T(8,128)S(1)}, f32[1152,128]{1,0:T(8,128)S(1)}, u32[]{:S(2)}, u32[]{:S(2)}) collective-permute-start(f32[1152,128]{1,0:T(8,128)S(1)} %get-tuple-element.61.cross_ref), channel_id=1, source_target_pairs={{29,26},{5,2},{13,10},{21,18}} | collective-permute-start | bytes 1769480 | tf_op jit(solution)/shard_map/ppermute | solution.py:509
  26.9 2.3 %copy-start.1 = (f32[2952,128]{1,0:T(8,128)S(1)}, f32[2952,128]{1,0:T(8,128)}, u32[]{:S(2)}) copy-start(f32[2952,128]{1,0:T(8,128)} %get-tuple-element.40.node) | copy-start | bytes 4534276
  26.9 3.4 %collective-permute-start.7 = (f32[648,128]{1,0:T(8,128)S(1)}, f32[648,128]{1,0:T(8,128)S(1)}, u32[]{:S(2)}, u32[]{:S(2)}) collective-permute-start(f32[648,128]{1,0:T(8,128)S(1)} %get-tuple-element.62), channel_id=1, source_target_pairs={{29,22},{5,30},{13,6},{21,14}} | collective-permute-start | bytes 995336 | tf_op jit(solution)/shard_map/ppermute | solution.py:509
  27.7 4.2 %collective-permute-start.12 = (f32[1296,128]{1,0:T(8,128)S(1)}, f32[1296,128]{1,0:T(8,128)S(1)}, u32[]{:S(2)}, u32[]{:S(2)}) collective-permute-start(f32[1296,128]{1,0:T(8,128)S(1)} %get-tuple-element.66), channel_id=1, source_target_pairs={{29,24},{5,0},{13,8},{21,16}} | collective-permute-start | bytes 1990664 | tf_op jit(solution)/shard_map/ppermute | solution.py:509
  28.5 4.8 %collective-permute-start.13 = (f32[1296,128]{1,0:T(8,128)S(1)}, f32[1296,128]{1,0:T(8,128)S(1)}, u32[]{:S(2)}, u32[]{:S(2)}) collective-permute-start(f32[1296,128]{1,0:T(8,128)S(1)} %get-tuple-element.67), channel_id=1, source_target_pairs={{29,26},{5,2},{13,10},{21,18}} | collective-permute-start | bytes 1990664 | tf_op jit(solution)/shard_map/ppermute | solution.py:509
  29.6 3.6 %collective-permute-start.11 = (f32[1152,128]{1,0:T(8,128)S(1)}, f32[1152,128]{1,0:T(8,128)S(1)}, u32[]{:S(2)}, u32[]{:S(2)}) collective-permute-start(f32[1152,128]{1,0:T(8,128)S(1)} %collective-permute-done.8.refs_2_), channel_id=1, source_target_pairs={{0,30},{8,6},{16,14},{24,22}} | collective-permute-start | bytes 1769480 | tf_op jit(solution)/shard_map/ppermute | solution.py:509
  30.4 4.2 %collective-permute-start.16 = (f32[2952,128]{1,0:T(8,128)S(1)}, f32[2952,128]{1,0:T(8,128)S(1)}, u32[]{:S(2)}, u32[]{:S(2)}) collective-permute-start(f32[2952,128]{1,0:T(8,128)S(1)} %collective-permute-done.4.came_node.refs_0_.refs_1_), channel_id=1, source_target_pairs={{31,28},{7,4},{15,12},{23,20}} | collective-permute-start | bytes 4534280 | tf_op jit(solution)/shard_map/ppermute | solution.py:509
  31.1 4.1 %collective-permute-start.15 = (f32[2448,128]{1,0:T(8,128)S(1)}, f32[2448,128]{1,0:T(8,128)S(1)}, u32[]{:S(2)}, u32[]{:S(2)}) collective-permute-start(f32[2448,128]{1,0:T(8,128)S(1)} %get-tuple-element.68), channel_id=1, source_target_pairs={{29,28},{5,4},{13,12},{21,20}} | collective-permute-start | bytes 3760136 | tf_op jit(solution)/shard_map/ppermute | solution.py:509
  31.9 18.8 %collective-permute-start.10 = (f32[1296,128]{1,0:T(8,128)S(1)}, f32[1296,128]{1,0:T(8,128)S(1)}, u32[]{:S(2)}, u32[]{:S(2)}) collective-permute-start(f32[1296,128]{1,0:T(8,128)S(1)} %early.1.refs_3_), channel_id=1, source_target_pairs={{30,31},{6,7},{14,15},{22,23},{0,1},{8,9},{16,17},{24,25},{2,3},{1... | collective-permute-start | bytes 1990664 | tf_op jit(solution)/shard_map/ppermute | solution.py:509
  33.3 23.8 %collective-permute-start.14 = (f32[1296,128]{1,0:T(8,128)S(1)}, f32[1296,128]{1,0:T(8,128)S(1)}, u32[]{:S(2)}, u32[]{:S(2)}) collective-permute-start(f32[1296,128]{1,0:T(8,128)S(1)} %late.1), channel_id=1, source_target_pairs={{30,31},{6,7},{14,15},{22,23},{0,1},{8,9},{16,17},{24,25},{2,3},{1... | collective-permute-start | bytes 1990664 | tf_op jit(solution)/shard_map/ppermute | solution.py:509
